TPU v7x, 32 devices: a whole 2x2x4 slice. The times are simulated.
32 devices in a mesh: row: 8 (over z, core), col: 4 (over y, x).
Axes of the slice: x: 2, y: 2, z: 4, core: 2. Of those that a mesh axis runs over, the one named last changes fastest.
Arguments:
- features: bfloat16 [4096, 128], P(('row', 'col')), may hold values from -6 to 6
- weight: bfloat16 [128, 256], replicated, may hold values from -0.5 to 0.5
- bias: float32 [256], replicated, may hold values from -3 to 3
- tiles: bfloat16 [8, 4, 8, 512, 512], P('row', 'col'), may hold values from -0.125 to 0.125
- tile_rows: int32 [8, 4, 8], P('row', 'col'), may hold values from 0 to 0
- tile_cols: int32 [8, 4, 8], P('row', 'col'), may hold values from 0 to 1
- tile_counts: int32 [8, 4], P('row', 'col'), may hold values from 1 to 8, as said below
- cotangent: bfloat16 [4096, 256], P(('row', 'col')), may hold values from -6 to 6
Outputs:
- output: bfloat16 [4096, 256], P(('row', 'col'))
- grad_features: bfloat16 [4096, 128], P(('row', 'col'))
- grad_weight: float32 [128, 256], replicated
- grad_bias: float32 [256], replicated
Inputs may be any that keep to these rules, and one draw needn't show every extreme that they name: `tile_counts`: some device has all 8 slots live.
All inputs are finite; a program needn't handle non-finite values.
Results may differ from a plain program's by a relative error of at most 0.02.
Values may be sent and summed in bfloat16 or wider, within the bound.
A program may use at most 64 MiB of HBM per device.

v0:
```python
import jax
import jax.numpy as jnp
from jax import lax
from jax.sharding import PartitionSpec as P


def shards(features, weight, bias, tiles, tile_rows, tile_cols, tile_counts, cotangent):
    tile_len = tiles.shape[3]
    slot_count = tiles.shape[2]
    hidden = weight.shape[1]
    my_tiles = tiles[0, 0]
    my_rows = tile_rows[0, 0]
    my_cols = tile_cols[0, 0]
    slot_ids = jnp.arange(slot_count, dtype=jnp.int32)
    is_live = (slot_ids < tile_counts[0, 0]).astype(jnp.float32)
    projected = jnp.dot(features, weight, preferred_element_type=jnp.float32).astype(jnp.bfloat16)
    panel = lax.all_gather(projected, "row", axis=0, tiled=True)
    col_tiles = panel.shape[0] // tile_len
    block_len = features.shape[0] * lax.axis_size("col")
    row_tiles = block_len // tile_len
    picked = panel.reshape(col_tiles, tile_len, hidden)[my_cols]
    product = jnp.einsum("ktj,kjh->kth", my_tiles, picked, preferred_element_type=jnp.float32)
    row_placer = (my_rows[:, None] == jnp.arange(row_tiles, dtype=jnp.int32)[None, :]).astype(
        jnp.float32
    ) * is_live[:, None]
    partial_value = jnp.einsum("kr,kth->rth", row_placer, product).reshape(block_len, hidden)
    partial_value = partial_value.astype(jnp.bfloat16).astype(jnp.float32)
    aggregate = lax.psum_scatter(
        partial_value.astype(jnp.bfloat16), "col", scatter_dimension=0, tiled=True
    ).astype(jnp.float32)
    pre_act = aggregate + bias
    sigmoid_val = jax.nn.sigmoid(pre_act)
    output = (pre_act * sigmoid_val).astype(jnp.bfloat16)
    derivative = sigmoid_val * (1.0 + pre_act * (1.0 - sigmoid_val))
    grad_pre = (cotangent.astype(jnp.float32) * derivative).astype(jnp.bfloat16)
    bias_local = jnp.sum(grad_pre.astype(jnp.float32), axis=0)
    grad_block = lax.all_gather(grad_pre, "col", axis=0, tiled=True)
    picked_back = grad_block.reshape(row_tiles, tile_len, hidden)[my_rows]
    back_product = jnp.einsum(
        "ktj,kth->kjh", my_tiles, picked_back, preferred_element_type=jnp.float32
    )
    col_placer = (my_cols[:, None] == jnp.arange(col_tiles, dtype=jnp.int32)[None, :]).astype(
        jnp.float32
    ) * is_live[:, None]
    back_partial = jnp.einsum("kr,kjh->rjh", col_placer, back_product).reshape(
        col_tiles * tile_len, hidden
    )
    back_partial = back_partial.astype(jnp.bfloat16).astype(jnp.float32)
    grad_projected = lax.psum_scatter(
        back_partial.astype(jnp.bfloat16), "row", scatter_dimension=0, tiled=True
    )
    grad_features = lax.dot_general(
        grad_projected, weight, (((1,), (1,)), ((), ())), preferred_element_type=jnp.float32
    ).astype(jnp.bfloat16)
    weight_local = lax.dot_general(
        features, grad_projected, (((0,), (0,)), ((), ())), preferred_element_type=jnp.float32
    )
    grad_weight, grad_bias = lax.psum((weight_local, bias_local), ("row", "col"))
    return (output, grad_features, grad_weight, grad_bias)


def solution(mesh):
    return jax.shard_map(
        shards,
        mesh=mesh,
        in_specs=(
            P(("row", "col"), None),
            P(),
            P(),
            P("row", "col", None, None, None),
            P("row", "col", None),
            P("row", "col", None),
            P("row", "col"),
            P(("row", "col"), None),
        ),
        out_specs=(P(("row", "col"), None), P(("row", "col"), None), P(), P()),
        check_vma=False,
    )
```

profile of v0, /device:TPU:0, one launch (start us, length us, event | category | flops | bytes accessed | tf_op | source)
XLA Modules:
  0.0 254.3 jit_solution(5335095557122648817)
XLA Ops:
  7.2 0.0 copy-start
  7.2 0.0 reduce-scatter.3.cloned.1.call-start
  7.9 0.7 fusion.19
  8.5 0.0 copy-done
  8.5 0.9 convolution_convert_fusion
  9.5 16.6 %all_gather.6 = bf16[1024,256]{1,0:T(8,128)(2,1)S(1)} all-gather(bf16[128,256]{1,0:T(8,128)(2,1)S(1)} %convolution_convert_fusion), channel_id=1, replica_groups=mesh['row'=8,'col'=4] {'row'}, dimensions={0}, use_global_device_ids=true | all-gather | bytes 589824 | tf_op jit(solution)/shard_map/all_gather | solution.py:17
  26.0 0.7 gather_fusion
  26.7 4.9 %fusion.6 = bf16[8,512,256]{1,2,0:T(8,128)(2,1)} fusion(bf16[8,512,256]{2,1,0:T(8,128)(2,1)S(1)} %gather_fusion, bf16[1,1,8,512,512]{4,3,2,1,0:T(8,128)(2,1)} %param.11), kind=kOutput, calls=%fused_computation.7 | convolution fusion | flops 1073741824 | bytes 8388608 | tf_op jit(solution)/shard_map/ktj,kjh->kth/dot_general | solution.py:22
  31.6 0.0 copy-start.4
  31.6 3.3 %copy.15 = bf16[8,512,256]{2,0,1:T(8,128)(2,1)S(1)} copy(bf16[8,512,256]{1,2,0:T(8,128)(2,1)} %fusion.6) | data formatting | bytes 4194304 | tf_op jit(solution)/shard_map/ktj,kjh->kth/dot_general | solution.py:22
  35.0 0.0 copy-start.2
  35.0 0.0 copy-start.3
  35.0 0.0 copy-done.4
  35.0 0.7 fusion.17
  35.7 0.7 copy.19
  36.4 0.0 reduce-scatter.3.cloned.1.call-update
  36.4 0.0 reduce-scatter.5.cloned.1.call-start
  36.5 25.2 %reduce-scatter.3.cloned.1.call-done = bf16[128,256]{1,0:T(8,128)(2,1)} async-done(((bf16[512,256]{1,0:T(8,128)(2,1)}), bf16[128,256]{1,0:T(8,128)(2,1)}) %reduce-scatter.3.cloned.1.call-update) | async-done | bytes 65552 | tf_op jit(solution)/shard_map/reduce_scatter | solution.py:28
  61.7 0.0 copy-done.2
  61.7 0.0 copy-done.3
  61.7 1.5 convert_reduce_fusion
  63.3 9.2 %all_gather.7 = bf16[512,256]{1,0:T(8,128)(2,1)S(1)} all-gather(bf16[128,256]{1,0:T(8,128)(2,1)S(1)} %get-tuple-element.13), channel_id=1, replica_groups=mesh['row'=8,'col'=4] {'col'}, dimensions={0}, use_global_device_ids=true | all-gather | bytes 327680 | tf_op jit(solution)/shard_map/all_gather | solution.py:37
  72.5 3.5 %fusion.2 = bf16[8,256,512]{2,1,0:T(8,128)(2,1)S(1)} fusion(bf16[1,1,8,512,512]{4,3,2,1,0:T(8,128)(2,1)} %param.11, bf16[512,256]{1,0:T(8,128)(2,1)S(1)} %all_gather.7), kind=kOutput, calls=%fused_computation.3 | convolution fusion | flops 1073741824 | bytes 6553600 | tf_op jit(solution)/shard_map/ktj,kth->kjh/dot_general | solution.py:39
  76.0 0.0 copy-start.5
  76.0 3.1 %copy.17 = bf16[8,256,512]{1,0,2:T(8,128)(2,1)} copy(bf16[8,256,512]{2,1,0:T(8,128)(2,1)S(1)} %fusion.2) | data formatting | bytes 4194304 | tf_op jit(solution)/shard_map/ktj,kth->kjh/dot_general | solution.py:39
  79.1 0.0 copy-done.5
  79.1 0.0 copy-start.1
  79.1 2.3 fusion.9
  81.4 0.9 copy.13
  82.2 0.0 reduce-scatter.5.cloned.1.call-update
  82.3 0.0 all-reduce.2.cloned.1.call-start
  82.3 39.4 %psum.15 = f32[256]{0:T(256)} all-reduce(f32[256]{0:T(256)S(1)} %get-tuple-element.12), channel_id=1, replica_groups=mesh['row'=8,'col'=4] {'row','col'}, use_global_device_ids=true, to_apply=%region_4.0 | all-reduce | flops 256 | bytes 2048 | tf_op jit(solution)/shard_map/psum | solution.py:58
  121.8 0.0 reduce-scatter.5.cloned.1.call-done
  121.8 0.0 copy-done.1
  121.8 1.7 convolution_bitcast_fusion
  123.4 0.0 all-reduce.2.cloned.1.call-update
  123.5 1.6 convolution_convert_fusion.1
  125.1 121.0 %all-reduce.2.cloned.1.call-done = f32[128,256]{0,1:T(8,128)} async-done(((f32[128,256]{0,1:T(8,128)}), f32[128,256]{0,1:T(8,128)}) %all-reduce.2.cloned.1.call-update) | async-done | bytes 131088 | tf_op jit(solution)/shard_map/psum | solution.py:58
  246.1 1.7 copy.14
  (2 shorter events, 0.0 us)
Async XLA Ops:
  7.2 1.4 copy-start
  7.2 54.5 %reduce-scatter.3.cloned.1.call-start = ((), (), s32[]{:S(2)}) async-start(), calls=%async_computation.2 | async-start | bytes 327680 | tf_op jit(solution)/shard_map/reduce_scatter | solution.py:28
  31.6 3.4 %copy-start.4 = (s32[1,1,8]{2,1,0:T(1,128)S(1)}, s32[1,1,8]{2,1,0:T(1,128)}, u32[]{:S(2)}) copy-start(s32[1,1,8]{2,1,0:T(1,128)} %param.12) | copy-start | bytes 100
  35.0 26.8 %copy-start.2 = (bf16[128,256]{1,0:T(8,128)(2,1)S(1)}, bf16[128,256]{1,0:T(8,128)(2,1)}, u32[]{:S(2)}) copy-start(bf16[128,256]{1,0:T(8,128)(2,1)} %param.15) | copy-start | bytes 196612
  35.0 26.8 %copy-start.3 = (f32[256]{0:T(256)S(1)}, f32[256]{0:T(256)}, u32[]{:S(2)}) copy-start(f32[256]{0:T(256)} %param.10) | copy-start | bytes 3076
  36.4 85.3 %reduce-scatter.5.cloned.1.call-start = ((), (), s32[]{:S(2)}) async-start(), calls=%async_computation.3 | async-start | bytes 589824 | tf_op jit(solution)/shard_map/reduce_scatter | solution.py:49
  76.0 3.1 %copy-start.5 = (s32[1,1,8]{2,1,0:T(1,128)S(1)}, s32[1,1,8]{2,1,0:T(1,128)}, u32[]{:S(2)}) copy-start(s32[1,1,8]{2,1,0:T(1,128)} %param.13) | copy-start | bytes 100
  79.1 42.7 %copy-start.1 = (bf16[128,128]{1,0:T(8,128)(2,1)S(1)}, bf16[128,128]{1,0:T(8,128)(2,1)}, u32[]{:S(2)}) copy-start(bf16[128,128]{1,0:T(8,128)(2,1)} %param.8) | copy-start | bytes 98308
  82.3 163.8 %all-reduce.2.cloned.1.call-start = ((), (), s32[]{:S(2)}) async-start(), calls=%async_computation.4 | async-start | bytes 262144 | tf_op jit(solution)/shard_map/psum | solution.py:58
Sparse Core Ops, SparseCore 0:
  36.6 25.1 reduce-scatter.2
  82.4 31.1 reduce-scatter.4
  123.6 122.4 all-reduce.1
where the time goes:
time: 255 us; the launch traced here: 254 us
  waiting for transfers between devices  146 us (57%)
  blocking collectives  65.3 us (26%)
  matrix products  15.5 us (6%)
  between operations  14.5 us (6%)
  local copies, waits for them, and re-layouts  10.4 us (4%)
    psum x1, waiting for transfers between devices, shards(): lax.psum((weight_local, bias_local), ('row', 'col'))  121 us
    psum x1, blocking collectives, shards(): lax.psum((weight_local, bias_local), ('row', 'col'))  39.4 us
    reduce_scatter x1, waiting for transfers between devices, shards(): lax.psum_scatter(partial_value.astype(jnp.bfloat16), 'col', scatter_dimen...  25.2 us
    all_gather x1, blocking collectives, shards(): panel = lax.all_gather(projected, 'row', axis=0, tiled=True)  16.6 us
    all_gather x1, blocking collectives, shards(): grad_block = lax.all_gather(grad_pre, 'col', axis=0, tiled=True)  9.24 us
  transfers between devices with their start and end apart: 3, of which 2 were waited for; matrix products, arithmetic and copies ran while one was open for 1% of the time, Pallas kernels for 0%

commit v1 on v0

v1 whole, which is shorter than its diff:
```python
import functools

import jax
import jax.numpy as jnp
from jax import lax
from jax.experimental import pallas as pl
from jax.experimental.pallas import tpu as pltpu
from jax.sharding import PartitionSpec as P

F32, BF16 = jnp.float32, jnp.bfloat16
EXTRA = 16
CHUNK = 16


def kernel(
    n_row, n_col, fused_weight,
    feat_hbm, weight_hbm, bias_hbm, tiles_hbm, rows_ref, cols_ref, counts_ref, cot_hbm,
    out_hbm, gf_hbm, gw_hbm, gb_hbm,
    tile_buf, adj, panel, weight, bias, cot, part, part_in, z_buf, back, back_in,
    gw_own, gw_in, gw_mid, gw_all, out_st, gf_st, gw_st, gb_st,
    tile_sem, load_sem, store_sem, send_sem, recv_sem,
):
    my_row, my_col = lax.axis_index("row"), lax.axis_index("col")
    nodes, feat = feat_hbm.shape
    hidden = weight.shape[1]
    slots, tile_len = tile_buf.shape[0], tile_buf.shape[1]
    row_tiles, col_tiles = adj.shape[0] // tile_len, adj.shape[1] // tile_len
    row_peers = [lax.rem(my_row + d, n_row) for d in range(1, n_row)]
    col_peers = [lax.rem(my_col + d, n_col) for d in range(1, n_col)]

    def at_row(peer):
        return (peer, my_col)

    def at_col(peer):
        return (my_row, peer)

    tile_parts = tile_sem.shape[0]
    part_rows = tile_len // tile_parts
    tile_loads = [
        pltpu.make_async_copy(
            tiles_hbm.at[0, 0, :, pl.ds(j * part_rows, part_rows), :],
            tile_buf.at[:, pl.ds(j * part_rows, part_rows), :],
            tile_sem.at[j],
        )
        for j in range(tile_parts)
    ]
    own_rows = pl.ds(pl.multiple_of(my_row * nodes, nodes), nodes)
    loads = [
        pltpu.make_async_copy(feat_hbm, panel.at[own_rows, :], load_sem.at[0]),
        pltpu.make_async_copy(weight_hbm, weight, load_sem.at[1]),
        pltpu.make_async_copy(bias_hbm, bias, load_sem.at[2]),
        pltpu.make_async_copy(cot_hbm, cot, load_sem.at[3]),
    ]
    barrier = pltpu.get_barrier_semaphore()
    for peer in row_peers:
        pl.semaphore_signal(barrier, inc=1, device_id=at_row(peer), device_id_type=pl.DeviceIdType.MESH)
    for peer in col_peers:
        pl.semaphore_signal(barrier, inc=1, device_id=at_col(peer), device_id_type=pl.DeviceIdType.MESH)
    for copy in tile_loads + loads:
        copy.start()
    pl.semaphore_wait(barrier, n_row + n_col - 2)

    def send(src, dst, phase, target):
        copy = pltpu.make_async_remote_copy(
            src_ref=src, dst_ref=dst, send_sem=send_sem.at[phase], recv_sem=recv_sem.at[phase],
            device_id=target, device_id_type=pl.DeviceIdType.MESH,
        )
        copy.start()

    def wait_in(ref, phase):
        pltpu.make_async_copy(ref, ref, recv_sem.at[phase]).wait()

    def wait_out(ref, phase):
        pltpu.make_async_copy(ref, ref, send_sem.at[phase]).wait()

    for peer in row_peers:
        send(feat_hbm, panel.at[own_rows, :], 0, at_row(peer))

    count = counts_ref[0, 0]
    group = 2 if col_tiles % 2 == 0 else 1
    groups = row_tiles * col_tiles // group

    def densify(tile_row, first_col, start, steps):
        gains = []
        for k in range(slots):
            live = jnp.logical_and(k < count, rows_ref[0, 0, k] == tile_row)
            col = cols_ref[0, 0, k]
            gains.append([
                jnp.where(jnp.logical_and(live, col == first_col + g), 1.0, 0.0).astype(F32)
                for g in range(group)
            ])

        def step(i, carry):
            at = pl.multiple_of(start + i * CHUNK, CHUNK)
            totals = [jnp.zeros((CHUNK, tile_len), F32) for _ in range(group)]
            for k in range(slots):
                block = tile_buf[k, pl.ds(at, CHUNK), :].astype(F32)
                totals = [total + block * gains[k][g] for g, total in enumerate(totals)]
            for g, total in enumerate(totals):
                rows = pl.ds(pl.multiple_of(tile_row * tile_len + at, CHUNK), CHUNK)
                lanes = pl.ds(pl.multiple_of((first_col + g) * tile_len, tile_len), tile_len)
                adj[rows, lanes] = total.astype(BF16)
            return carry

        lax.fori_loop(0, steps, step, 0)

    if groups == 1:
        for j in range(tile_parts):
            tile_loads[j].wait()
            densify(0, 0, j * part_rows, part_rows // CHUNK)
    else:
        for j in range(tile_parts):
            tile_loads[j].wait()

        def one_group(i, carry):
            per_row = col_tiles // group
            densify(i // per_row, lax.rem(i, per_row) * group, 0, tile_len // CHUNK)
            return carry

        lax.fori_loop(0, groups, one_group, 0)

    for copy in loads:
        copy.wait()
    wait_in(panel.at[pl.ds(0, (n_row - 1) * nodes), :], 0)
    for c in range(n_col):
        part[c] = jnp.dot(
            adj[c * nodes:(c + 1) * nodes, :], panel[...], preferred_element_type=F32
        ).astype(BF16)
    for peer in col_peers:
        send(part.at[peer], part_in.at[my_col], 1, at_col(peer))
    part_in[my_col] = part[my_col]
    wait_in(part_in.at[pl.ds(0, n_col - 1)], 1)
    mixed = part_in[0].astype(F32)
    for c in range(1, n_col):
        mixed = mixed + part_in[c].astype(F32)
    mixed = mixed.astype(BF16)

    pre_act = jnp.dot(mixed, weight[...], preferred_element_type=F32) + bias[...]
    sig = jax.nn.sigmoid(pre_act)
    grad_pre = (cot[...].astype(F32) * (sig * (1.0 + pre_act * (1.0 - sig)))).astype(BF16)
    z_own = lax.dot_general(weight[...], grad_pre, (((1,), (1,)), ((), ())), preferred_element_type=F32)
    own_lanes = pl.ds(pl.multiple_of(my_col * nodes, nodes), nodes)
    z_buf[0:feat, own_lanes] = z_own.astype(BF16)
    gb_local = jnp.sum(grad_pre.astype(F32), axis=0, keepdims=True)
    halves = [gb_local[:, i * nodes:(i + 1) * nodes] for i in range(hidden // nodes)]
    n_half = len(halves)
    high = [half.astype(BF16).astype(F32) for half in halves]
    low = [half - top for half, top in zip(halves, high)]
    pad = jnp.zeros((EXTRA - 2 * n_half, nodes), F32)
    z_buf[feat:feat + EXTRA, own_lanes] = jnp.concatenate(high + low + [pad], axis=0).astype(BF16)
    for peer in col_peers:
        send(z_buf.at[:, own_lanes], z_buf.at[:, own_lanes], 2, at_col(peer))
    gw_local = lax.dot_general(mixed, grad_pre, (((0,), (0,)), ((), ())), preferred_element_type=F32)
    if fused_weight:
        share = feat // n_row
        gw_own[...] = gw_local.astype(BF16).reshape(n_row, share, hidden)
        for peer in row_peers:
            send(gw_own.at[peer], gw_in.at[my_row], 4, at_row(peer))
        gw_in[my_row] = gw_own[my_row]
    else:
        gw_st[...] = gw_local
    out_st[...] = (pre_act * sig).astype(BF16)
    out_store = pltpu.make_async_copy(out_st, out_hbm, store_sem.at[0])
    out_store.start()

    wait_in(z_buf.at[:, pl.ds(0, (n_col - 1) * nodes)], 2)
    gb_block = z_buf[feat:feat + EXTRA, 0:nodes].astype(F32)
    for c in range(1, n_col):
        gb_block = gb_block + z_buf[feat:feat + EXTRA, c * nodes:(c + 1) * nodes].astype(F32)
    halves = [gb_block[i:i + 1, :] + gb_block[n_half + i:n_half + i + 1, :] for i in range(n_half)]
    high = [half.astype(BF16).astype(F32) for half in halves]
    low = [half - top for half, top in zip(halves, high)]
    gb_rows = jnp.concatenate(high + low + [pad], axis=0).astype(BF16)
    for r in range(n_row):
        back[r, 0:feat, :] = jnp.dot(
            z_buf[0:feat, :], adj[:, r * nodes:(r + 1) * nodes], preferred_element_type=F32
        ).astype(BF16)
        back[r, feat:feat + EXTRA, :] = gb_rows
    for peer in row_peers:
        send(back.at[peer], back_in.at[my_row], 3, at_row(peer))
    back_in[my_row] = back[my_row]

    if fused_weight:
        wait_in(gw_in.at[pl.ds(0, n_row - 1)], 4)
        gw_sum = gw_in[0].astype(F32)
        for r in range(1, n_row):
            gw_sum = gw_sum + gw_in[r].astype(F32)
        gw_mid[my_col] = gw_sum.astype(BF16)
        for peer in col_peers:
            send(gw_mid.at[my_col], gw_mid.at[my_col], 5, at_col(peer))
        wait_in(gw_mid.at[pl.ds(0, n_col - 1)], 5)
        gw_sum = gw_mid[0].astype(F32)
        for c in range(1, n_col):
            gw_sum = gw_sum + gw_mid[c].astype(F32)
        gw_all[my_row] = gw_sum.astype(BF16)
        for peer in row_peers:
            send(gw_all.at[my_row], gw_all.at[my_row], 6, at_row(peer))

    wait_in(back_in.at[pl.ds(0, n_row - 1)], 3)
    total = back_in[0].astype(F32)
    for r in range(1, n_row):
        total = total + back_in[r].astype(F32)
    gf_st[...] = total[0:feat, :].T.astype(BF16)
    gf_store = pltpu.make_async_copy(gf_st, gf_hbm, store_sem.at[1])
    gf_store.start()
    for i in range(n_half):
        gb_st[:, i * nodes:(i + 1) * nodes] = (
            total[feat + i:feat + i + 1, :] + total[feat + n_half + i:feat + n_half + i + 1, :]
        )
    gb_store = pltpu.make_async_copy(gb_st, gb_hbm, store_sem.at[2])
    gb_store.start()
    if fused_weight:
        wait_in(gw_all.at[pl.ds(0, n_row - 1)], 6)
        gw_st[...] = gw_all[...].astype(F32).reshape(feat, hidden)
    gw_store = pltpu.make_async_copy(gw_st, gw_hbm, store_sem.at[3])
    gw_store.start()

    wait_out(panel.at[pl.ds(0, (n_row - 1) * nodes), :], 0)
    wait_out(part_in.at[pl.ds(0, n_col - 1)], 1)
    wait_out(z_buf.at[:, pl.ds(0, (n_col - 1) * nodes)], 2)
    wait_out(back_in.at[pl.ds(0, n_row - 1)], 3)
    if fused_weight:
        wait_out(gw_in.at[pl.ds(0, n_row - 1)], 4)
        wait_out(gw_mid.at[pl.ds(0, n_col - 1)], 5)
        wait_out(gw_all.at[pl.ds(0, n_row - 1)], 6)
    for store in (out_store, gf_store, gb_store, gw_store):
        store.wait()


def shards(n_row, n_col, features, weight, bias, tiles, tile_rows, tile_cols, tile_counts, cotangent):
    nodes, feat = features.shape
    hidden = weight.shape[1]
    slots, tile_len = tiles.shape[2], tiles.shape[3]
    block_len, panel_len = nodes * n_col, nodes * n_row
    fused_weight = feat % (n_row * 16) == 0
    share = feat // n_row if fused_weight else 16
    hbm = pl.BlockSpec(memory_space=pl.ANY)
    smem = pl.BlockSpec(memory_space=pltpu.SMEM)
    out, gf, gw, gb = pl.pallas_call(
        functools.partial(kernel, n_row, n_col, fused_weight),
        out_shape=(
            jax.ShapeDtypeStruct((nodes, hidden), BF16),
            jax.ShapeDtypeStruct((nodes, feat), BF16),
            jax.ShapeDtypeStruct((feat, hidden), F32),
            jax.ShapeDtypeStruct((1, hidden), F32),
        ),
        in_specs=[hbm, hbm, hbm, hbm, smem, smem, smem, hbm],
        out_specs=(hbm, hbm, hbm, hbm),
        scratch_shapes=[
            pltpu.VMEM((slots, tile_len, tile_len), BF16),
            pltpu.VMEM((block_len, panel_len), BF16),
            pltpu.VMEM((panel_len, feat), BF16),
            pltpu.VMEM((feat, hidden), BF16),
            pltpu.VMEM((1, hidden), F32),
            pltpu.VMEM((nodes, hidden), BF16),
            pltpu.VMEM((n_col, nodes, feat), BF16),
            pltpu.VMEM((n_col, nodes, feat), BF16),
            pltpu.VMEM((feat + EXTRA, block_len), BF16),
            pltpu.VMEM((n_row, feat + EXTRA, nodes), BF16),
            pltpu.VMEM((n_row, feat + EXTRA, nodes), BF16),
            pltpu.VMEM((n_row, share, hidden), BF16),
            pltpu.VMEM((n_row, share, hidden), BF16),
            pltpu.VMEM((n_col, share, hidden), BF16),
            pltpu.VMEM((n_row, share, hidden), BF16),
            pltpu.VMEM((nodes, hidden), BF16),
            pltpu.VMEM((nodes, feat), BF16),
            pltpu.VMEM((feat, hidden), F32),
            pltpu.VMEM((1, hidden), F32),
            pltpu.SemaphoreType.DMA((4,)),
            pltpu.SemaphoreType.DMA((4,)),
            pltpu.SemaphoreType.DMA((4,)),
            pltpu.SemaphoreType.DMA((7,)),
            pltpu.SemaphoreType.DMA((7,)),
        ],
        compiler_params=pltpu.CompilerParams(
            collective_id=0, has_side_effects=True, vmem_limit_bytes=48 * 1024 * 1024
        ),
    )(features, weight, bias.reshape(1, hidden), tiles, tile_rows, tile_cols, tile_counts, cotangent)
    gb = gb.reshape(hidden)
    if not fused_weight:
        gw = lax.psum(gw, ("row", "col"))
    return out, gf, gw, gb


def solution(mesh):
    return jax.shard_map(
        functools.partial(shards, mesh.shape["row"], mesh.shape["col"]),
        mesh=mesh,
        in_specs=(
            P(("row", "col"), None),
            P(),
            P(),
            P("row", "col", None, None, None),
            P("row", "col", None),
            P("row", "col", None),
            P("row", "col"),
            P(("row", "col"), None),
        ),
        out_specs=(P(("row", "col"), None), P(("row", "col"), None), P(), P()),
        check_vma=False,
    )
```

time: 255 us -> 40.4 us (0.16)
  waiting for transfers between devices: 146 us -> 0 us
  blocking collectives: 65.3 us -> 0 us
  Pallas kernels: 0 us -> 29.7 us
  matrix products: 15.5 us -> 0 us
  between operations: 14.5 us -> 1.3 us
    psum x1 -> x0, waiting for transfers between devices: 121 us -> none  [shards(): lax.psum((weight_local, bias_local), ('row', 'col'))]
    psum x1 -> x0, blocking collectives: 39.4 us -> none  [shards(): lax.psum((weight_local, bias_local), ('row', 'col'))]
    pallas_call x0 -> x1, Pallas kernels: none -> 29.7 us  [shards(): pl.pallas_call(functools.partial(kernel, n_row, n_col, fused_weight), out...]
    all_gather x2 -> x0, blocking collectives: 25.8 us -> none  [the longest x1 16.6 us: shards(): panel = lax.all_gather(projected, 'row', axis=0, tiled=True)]
    reduce_scatter x2 -> x0, waiting for transfers between devices: 25.2 us -> none  [the longest x1 25.2 us: shards(): lax.psum_scatter(partial_value.astype(jnp.bfloat16), 'col', scatter_dimen...]
    dot_general x7 -> x0, matrix products: 15.5 us -> none  [the longest x1 4.88 us: shards(): jnp.einsum('ktj,kjh->kth', my_tiles, picked, preferred_element_type=jnp.f...]
    unnamed x13 -> x18, local copies, waits for them, and re-layouts: 1.69 us -> 9.07 us
    dot_general x3 -> x0, local copies, waits for them, and re-layouts: 7.14 us -> none  [the longest x1 3.35 us: shards(): jnp.einsum('ktj,kjh->kth', my_tiles, picked, preferred_element_type=jnp.f...]
  transfers between devices with their start and end apart: 3 -> 0, of which waited for: 2 -> 0; matrix products, arithmetic and copies ran while one was open for 1% -> 0% of each run, Pallas kernels for 0% -> 0%
where the time goes in v1:
time: 40.4 us; the launch traced here: 40.1 us
  Pallas kernels  29.7 us (74%)
  local copies, waits for them, and re-layouts  9.07 us (22%)
  between operations  1.3 us (3%)
    pallas_call x1, Pallas kernels, shards(): pl.pallas_call(functools.partial(kernel, n_row, n_col, fused_weight), out...  29.7 us
    unnamed x18, local copies, waits for them, and re-layouts  9.07 us

profile of v1, /device:TPU:0, one launch (start us, length us, event | category | flops | bytes accessed | tf_op | source)
XLA Modules:
  0.0 40.1 jit_solution(3142950153783916896)
XLA Ops:
  1.3 0.0 copy-start
  1.3 2.2 %copy-done = bf16[1,1,8,512,512]{4,3,2,1,0:T(8,128)(2,1)S(1)} copy-done((bf16[1,1,8,512,512]{4,3,2,1,0:T(8,128)(2,1)S(1)}, bf16[1,1,8,512,512]{4,3,2,1,0:T(8,128)(2,1)}, u32[]{:S(2)}) %copy-start) | copy-done | bytes 4194328
  3.5 0.0 copy-start.1
  3.5 0.8 %copy-done.1 = bf16[128,256]{1,0:T(8,128)(2,1)S(1)} copy-done((bf16[128,256]{1,0:T(8,128)(2,1)S(1)}, bf16[128,256]{1,0:T(8,128)(2,1)}, u32[]{:S(2)}) %copy-start.1) | copy-done | bytes 65560
  4.3 0.0 copy-start.2
  4.3 0.8 %copy-done.2 = bf16[128,256]{1,0:T(8,128)(2,1)S(1)} copy-done((bf16[128,256]{1,0:T(8,128)(2,1)S(1)}, bf16[128,256]{1,0:T(8,128)(2,1)}, u32[]{:S(2)}) %copy-start.2) | copy-done | bytes 65560
  5.1 0.0 copy-start.3
  5.2 0.8 %copy-done.3 = bf16[128,128]{1,0:T(8,128)(2,1)S(1)} copy-done((bf16[128,128]{1,0:T(8,128)(2,1)S(1)}, bf16[128,128]{1,0:T(8,128)(2,1)}, u32[]{:S(2)}) %copy-start.3) | copy-done | bytes 32792
  5.9 0.0 copy-start.4
  5.9 0.7 %copy-done.4 = f32[256]{0:T(256)S(1)} copy-done((f32[256]{0:T(256)S(1)}, f32[256]{0:T(256)}, u32[]{:S(2)}) %copy-start.4) | copy-done | bytes 1048
  6.6 0.0 copy-start.5
  6.6 0.7 %copy-done.5 = s32[1,1,8]{2,1,0:T(1,128)S(1)} copy-done((s32[1,1,8]{2,1,0:T(1,128)S(1)}, s32[1,1,8]{2,1,0:T(1,128)}, u32[]{:S(2)}) %copy-start.5) | copy-done | bytes 56
  7.2 0.0 copy-start.6
  7.2 0.7 %copy-done.6 = s32[1,1,8]{2,1,0:T(1,128)S(1)} copy-done((s32[1,1,8]{2,1,0:T(1,128)S(1)}, s32[1,1,8]{2,1,0:T(1,128)}, u32[]{:S(2)}) %copy-start.6) | copy-done | bytes 56
  7.9 29.7 %shard_map.111 = (bf16[128,256]{1,0:T(8,128)(2,1)S(1)}, bf16[128,128]{1,0:T(8,128)(2,1)S(1)}, f32[128,256]{1,0:T(8,128)S(1)}, f32[1,256]{1,0:T(1,128)S(1)}) custom-call(bf16[128,128]{1,0:T(8,128)(2,1)S(1)} %copy-done.3, bf16[128,256]{1,0:T(8,128)(2,1)S(1)} %copy-done.1, f32[1,256]{1,0:T(1,128)S(1)} %bitcast.3, bf16[1,1,8,512,512]{4,3,2,1,0:T(8,128)(2,1)S(1)} %copy-done, ...), custom_call_target="tpu_custom_call" | custom-call | tf_op jit(solution)/shard_map/pallas_call | solution.py:239
  37.6 0.6 %copy.17 = bf16[128,256]{1,0:T(8,128)(2,1)} copy(bf16[128,256]{1,0:T(8,128)(2,1)S(1)} %get-tuple-element.16) | data formatting | bytes 131072
  38.3 0.6 %copy.18 = bf16[128,128]{1,0:T(8,128)(2,1)} copy(bf16[128,128]{1,0:T(8,128)(2,1)S(1)} %get-tuple-element.17) | data formatting | bytes 65536
  38.9 0.7 %copy.19 = f32[128,256]{1,0:T(8,128)} copy(f32[128,256]{1,0:T(8,128)S(1)} %get-tuple-element.18) | data formatting | bytes 262144
  39.5 0.6 %copy.20 = f32[256]{0:T(256)} copy(f32[256]{0:T(256)S(1)} %bitcast.2) | data formatting | bytes 2048
Async XLA Ops:
  1.3 2.2 %copy-start = (bf16[1,1,8,512,512]{4,3,2,1,0:T(8,128)(2,1)S(1)}, bf16[1,1,8,512,512]{4,3,2,1,0:T(8,128)(2,1)}, u32[]{:S(2)}) copy-start(bf16[1,1,8,512,512]{4,3,2,1,0:T(8,128)(2,1)} %tiles_hbm.1) | copy-start | bytes 12582916
  3.5 0.8 %copy-start.1 = (bf16[128,256]{1,0:T(8,128)(2,1)S(1)}, bf16[128,256]{1,0:T(8,128)(2,1)}, u32[]{:S(2)}) copy-start(bf16[128,256]{1,0:T(8,128)(2,1)} %weight_hbm.1) | copy-start | bytes 196612
  4.3 0.8 %copy-start.2 = (bf16[128,256]{1,0:T(8,128)(2,1)S(1)}, bf16[128,256]{1,0:T(8,128)(2,1)}, u32[]{:S(2)}) copy-start(bf16[128,256]{1,0:T(8,128)(2,1)} %cot_hbm.1) | copy-start | bytes 196612
  5.1 0.8 %copy-start.3 = (bf16[128,128]{1,0:T(8,128)(2,1)S(1)}, bf16[128,128]{1,0:T(8,128)(2,1)}, u32[]{:S(2)}) copy-start(bf16[128,128]{1,0:T(8,128)(2,1)} %feat_hbm.1) | copy-start | bytes 98308
  5.9 0.7 %copy-start.4 = (f32[256]{0:T(256)S(1)}, f32[256]{0:T(256)}, u32[]{:S(2)}) copy-start(f32[256]{0:T(256)} %param.10) | copy-start | bytes 3076
  6.6 0.7 %copy-start.5 = (s32[1,1,8]{2,1,0:T(1,128)S(1)}, s32[1,1,8]{2,1,0:T(1,128)}, u32[]{:S(2)}) copy-start(s32[1,1,8]{2,1,0:T(1,128)} %rows_ref.1) | copy-start | bytes 100
  7.2 0.7 %copy-start.6 = (s32[1,1,8]{2,1,0:T(1,128)S(1)}, s32[1,1,8]{2,1,0:T(1,128)}, u32[]{:S(2)}) copy-start(s32[1,1,8]{2,1,0:T(1,128)} %cols_ref.1) | copy-start | bytes 100

commit v2 on v1

--- a/solution.py
+++ b/solution.py
@@ -14,11 +14,11 @@
 
 def kernel(
     n_row, n_col, fused_weight,
-    feat_hbm, weight_hbm, bias_hbm, tiles_hbm, rows_ref, cols_ref, counts_ref, cot_hbm,
-    out_hbm, gf_hbm, gw_hbm, gb_hbm,
+    feat_hbm, weight_hbm, bias_hbm, tiles_hbm, rows_hbm, cols_hbm, counts_ref, cot_hbm,
+    out_st, gf_st, gw_st, gb_st,
     tile_buf, adj, panel, weight, bias, cot, part, part_in, z_buf, back, back_in,
-    gw_own, gw_in, gw_mid, gw_all, out_st, gf_st, gw_st, gb_st,
-    tile_sem, load_sem, store_sem, send_sem, recv_sem,
+    pair_in, back_out, gw_own, gw_in, gw_mid, gw_all,
+    rows_ref, cols_ref, tile_sem, load_sem, send_sem, recv_sem, hop_sem,
 ):
     my_row, my_col = lax.axis_index("row"), lax.axis_index("col")
     nodes, feat = feat_hbm.shape
@@ -27,6 +27,12 @@
     row_tiles, col_tiles = adj.shape[0] // tile_len, adj.shape[1] // tile_len
     row_peers = [lax.rem(my_row + d, n_row) for d in range(1, n_row)]
     col_peers = [lax.rem(my_col + d, n_col) for d in range(1, n_col)]
+
+    pairs = n_row // 2
+    pair, side = my_row // 2, lax.rem(my_row, 2)
+    other = 1 - side
+    sibling = pair * 2 + other
+    pair_peers = [lax.rem(pair + d, pairs) for d in range(1, pairs)]
 
     def at_row(peer):
         return (peer, my_col)
@@ -51,18 +57,23 @@
         pltpu.make_async_copy(bias_hbm, bias, load_sem.at[2]),
         pltpu.make_async_copy(cot_hbm, cot, load_sem.at[3]),
     ]
+    slot_loads = [
+        pltpu.make_async_copy(rows_hbm, rows_ref, load_sem.at[4]),
+        pltpu.make_async_copy(cols_hbm, cols_ref, load_sem.at[5]),
+    ]
     barrier = pltpu.get_barrier_semaphore()
     for peer in row_peers:
         pl.semaphore_signal(barrier, inc=1, device_id=at_row(peer), device_id_type=pl.DeviceIdType.MESH)
     for peer in col_peers:
         pl.semaphore_signal(barrier, inc=1, device_id=at_col(peer), device_id_type=pl.DeviceIdType.MESH)
-    for copy in tile_loads + loads:
+    for copy in slot_loads + tile_loads + loads:
         copy.start()
     pl.semaphore_wait(barrier, n_row + n_col - 2)
 
-    def send(src, dst, phase, target):
+    def send(src, dst, phase, target, landed=None):
         copy = pltpu.make_async_remote_copy(
-            src_ref=src, dst_ref=dst, send_sem=send_sem.at[phase], recv_sem=recv_sem.at[phase],
+            src_ref=src, dst_ref=dst, send_sem=send_sem.at[phase],
+            recv_sem=recv_sem.at[phase] if landed is None else landed,
             device_id=target, device_id_type=pl.DeviceIdType.MESH,
         )
         copy.start()
@@ -73,9 +84,12 @@
     def wait_out(ref, phase):
         pltpu.make_async_copy(ref, ref, send_sem.at[phase]).wait()
 
-    for peer in row_peers:
-        send(feat_hbm, panel.at[own_rows, :], 0, at_row(peer))
-
+    for d, peer in enumerate(pair_peers):
+        send(feat_hbm, panel.at[own_rows, :], 0, at_row(peer * 2 + side), hop_sem.at[d])
+    send(feat_hbm, panel.at[own_rows, :], 7, at_row(sibling))
+
+    for copy in slot_loads:
+        copy.wait()
     count = counts_ref[0, 0]
     group = 2 if col_tiles % 2 == 0 else 1
     groups = row_tiles * col_tiles // group
@@ -121,7 +135,12 @@
 
     for copy in loads:
         copy.wait()
-    wait_in(panel.at[pl.ds(0, (n_row - 1) * nodes), :], 0)
+    for d in range(pairs - 1):
+        source = lax.rem(pair + pairs - 1 - d, pairs) * 2 + side
+        block = panel.at[pl.ds(pl.multiple_of(source * nodes, nodes), nodes), :]
+        pltpu.make_async_copy(block, block, hop_sem.at[d]).wait()
+        send(block, block, 7, at_row(sibling))
+    wait_in(panel.at[pl.ds(0, pairs * nodes), :], 7)
     for c in range(n_col):
         part[c] = jnp.dot(
             adj[c * nodes:(c + 1) * nodes, :], panel[...], preferred_element_type=F32
@@ -160,25 +179,23 @@
     else:
         gw_st[...] = gw_local
     out_st[...] = (pre_act * sig).astype(BF16)
-    out_store = pltpu.make_async_copy(out_st, out_hbm, store_sem.at[0])
-    out_store.start()
 
     wait_in(z_buf.at[:, pl.ds(0, (n_col - 1) * nodes)], 2)
     gb_block = z_buf[feat:feat + EXTRA, 0:nodes].astype(F32)
     for c in range(1, n_col):
         gb_block = gb_block + z_buf[feat:feat + EXTRA, c * nodes:(c + 1) * nodes].astype(F32)
-    halves = [gb_block[i:i + 1, :] + gb_block[n_half + i:n_half + i + 1, :] for i in range(n_half)]
-    high = [half.astype(BF16).astype(F32) for half in halves]
-    low = [half - top for half, top in zip(halves, high)]
-    gb_rows = jnp.concatenate(high + low + [pad], axis=0).astype(BF16)
+    def split_rows(block):
+        tops = [block[i:i + 1, :] + block[n_half + i:n_half + i + 1, :] for i in range(n_half)]
+        rounded = [top.astype(BF16).astype(F32) for top in tops]
+        rest = [top - near for top, near in zip(tops, rounded)]
+        return jnp.concatenate(rounded + rest + [pad], axis=0).astype(BF16)
+
     for r in range(n_row):
-        back[r, 0:feat, :] = jnp.dot(
+        back[r % 2, r // 2, 0:feat, :] = jnp.dot(
             z_buf[0:feat, :], adj[:, r * nodes:(r + 1) * nodes], preferred_element_type=F32
         ).astype(BF16)
-        back[r, feat:feat + EXTRA, :] = gb_rows
-    for peer in row_peers:
-        send(back.at[peer], back_in.at[my_row], 3, at_row(peer))
-    back_in[my_row] = back[my_row]
+        back[r % 2, r // 2, feat:feat + EXTRA, :] = split_rows(gb_block)
+    send(back.at[other], pair_in, 8, at_row(sibling))
 
     if fused_weight:
         wait_in(gw_in.at[pl.ds(0, n_row - 1)], 4)
@@ -188,6 +205,17 @@
         gw_mid[my_col] = gw_sum.astype(BF16)
         for peer in col_peers:
             send(gw_mid.at[my_col], gw_mid.at[my_col], 5, at_col(peer))
+    wait_in(pair_in, 8)
+    back_out[:, 0:feat, :] = (
+        back[side, :, 0:feat, :].astype(F32) + pair_in[:, 0:feat, :].astype(F32)
+    ).astype(BF16)
+    gb_pair = split_rows(gb_block + pair_in[0, feat:feat + EXTRA, :].astype(F32))
+    for m in range(pairs):
+        back_out[m, feat:feat + EXTRA, :] = gb_pair
+    for peer in pair_peers:
+        send(back_out.at[peer], back_in.at[pair], 3, at_row(peer * 2 + side))
+    back_in[pair] = back_out[pair]
+    if fused_weight:
         wait_in(gw_mid.at[pl.ds(0, n_col - 1)], 5)
         gw_sum = gw_mid[0].astype(F32)
         for c in range(1, n_col):
@@ -196,35 +224,29 @@
         for peer in row_peers:
             send(gw_all.at[my_row], gw_all.at[my_row], 6, at_row(peer))
 
-    wait_in(back_in.at[pl.ds(0, n_row - 1)], 3)
+    wait_in(back_in.at[pl.ds(0, pairs - 1)], 3)
     total = back_in[0].astype(F32)
-    for r in range(1, n_row):
+    for r in range(1, pairs):
         total = total + back_in[r].astype(F32)
     gf_st[...] = total[0:feat, :].T.astype(BF16)
-    gf_store = pltpu.make_async_copy(gf_st, gf_hbm, store_sem.at[1])
-    gf_store.start()
     for i in range(n_half):
         gb_st[:, i * nodes:(i + 1) * nodes] = (
             total[feat + i:feat + i + 1, :] + total[feat + n_half + i:feat + n_half + i + 1, :]
         )
-    gb_store = pltpu.make_async_copy(gb_st, gb_hbm, store_sem.at[2])
-    gb_store.start()
     if fused_weight:
         wait_in(gw_all.at[pl.ds(0, n_row - 1)], 6)
         gw_st[...] = gw_all[...].astype(F32).reshape(feat, hidden)
-    gw_store = pltpu.make_async_copy(gw_st, gw_hbm, store_sem.at[3])
-    gw_store.start()
-
-    wait_out(panel.at[pl.ds(0, (n_row - 1) * nodes), :], 0)
+
+    wait_out(panel.at[pl.ds(0, (pairs - 1) * nodes), :], 0)
+    wait_out(panel.at[pl.ds(0, pairs * nodes), :], 7)
     wait_out(part_in.at[pl.ds(0, n_col - 1)], 1)
     wait_out(z_buf.at[:, pl.ds(0, (n_col - 1) * nodes)], 2)
-    wait_out(back_in.at[pl.ds(0, n_row - 1)], 3)
+    wait_out(back_in.at[pl.ds(0, pairs - 1)], 3)
+    wait_out(pair_in, 8)
     if fused_weight:
         wait_out(gw_in.at[pl.ds(0, n_row - 1)], 4)
         wait_out(gw_mid.at[pl.ds(0, n_col - 1)], 5)
         wait_out(gw_all.at[pl.ds(0, n_row - 1)], 6)
-    for store in (out_store, gf_store, gb_store, gw_store):
-        store.wait()
 
 
 def shards(n_row, n_col, features, weight, bias, tiles, tile_rows, tile_cols, tile_counts, cotangent):
@@ -234,8 +256,8 @@
     block_len, panel_len = nodes * n_col, nodes * n_row
     fused_weight = feat % (n_row * 16) == 0
     share = feat // n_row if fused_weight else 16
-    hbm = pl.BlockSpec(memory_space=pl.ANY)
-    smem = pl.BlockSpec(memory_space=pltpu.SMEM)
+    hbm = pl.BlockSpec(memory_space=pltpu.HBM)
+    vmem = pl.BlockSpec(memory_space=pltpu.VMEM)
     out, gf, gw, gb = pl.pallas_call(
         functools.partial(kernel, n_row, n_col, fused_weight),
         out_shape=(
@@ -244,8 +266,8 @@
             jax.ShapeDtypeStruct((feat, hidden), F32),
             jax.ShapeDtypeStruct((1, hidden), F32),
         ),
-        in_specs=[hbm, hbm, hbm, hbm, smem, smem, smem, hbm],
-        out_specs=(hbm, hbm, hbm, hbm),
+        in_specs=[hbm] * 6 + [pl.BlockSpec(memory_space=pltpu.SMEM), hbm],
+        out_specs=(vmem,) * 4,
         scratch_shapes=[
             pltpu.VMEM((slots, tile_len, tile_len), BF16),
             pltpu.VMEM((block_len, panel_len), BF16),
@@ -256,26 +278,33 @@
             pltpu.VMEM((n_col, nodes, feat), BF16),
             pltpu.VMEM((n_col, nodes, feat), BF16),
             pltpu.VMEM((feat + EXTRA, block_len), BF16),
-            pltpu.VMEM((n_row, feat + EXTRA, nodes), BF16),
-            pltpu.VMEM((n_row, feat + EXTRA, nodes), BF16),
+            pltpu.VMEM((2, n_row // 2, feat + EXTRA, nodes), BF16),
+            pltpu.VMEM((n_row // 2, feat + EXTRA, nodes), BF16),
+            pltpu.VMEM((n_row // 2, feat + EXTRA, nodes), BF16),
+            pltpu.VMEM((n_row // 2, feat + EXTRA, nodes), BF16),
             pltpu.VMEM((n_row, share, hidden), BF16),
             pltpu.VMEM((n_row, share, hidden), BF16),
             pltpu.VMEM((n_col, share, hidden), BF16),
             pltpu.VMEM((n_row, share, hidden), BF16),
-            pltpu.VMEM((nodes, hidden), BF16),
-            pltpu.VMEM((nodes, feat), BF16),
-            pltpu.VMEM((feat, hidden), F32),
-            pltpu.VMEM((1, hidden), F32),
+            pltpu.SMEM(tile_rows.shape, jnp.int32),
+            pltpu.SMEM(tile_cols.shape, jnp.int32),
             pltpu.SemaphoreType.DMA((4,)),
-            pltpu.SemaphoreType.DMA((4,)),
-            pltpu.SemaphoreType.DMA((4,)),
-            pltpu.SemaphoreType.DMA((7,)),
-            pltpu.SemaphoreType.DMA((7,)),
+            pltpu.SemaphoreType.DMA((6,)),
+            pltpu.SemaphoreType.DMA((9,)),
+            pltpu.SemaphoreType.DMA((9,)),
+            pltpu.SemaphoreType.DMA((n_row // 2,)),
         ],
         compiler_params=pltpu.CompilerParams(
             collective_id=0, has_side_effects=True, vmem_limit_bytes=48 * 1024 * 1024
         ),
-    )(features, weight, bias.reshape(1, hidden), tiles, tile_rows, tile_cols, tile_counts, cotangent)
+    )(
+        *[
+            pltpu.with_memory_space_constraint(x, pltpu.HBM)
+            for x in (features, weight, bias.reshape(1, hidden), tiles, tile_rows, tile_cols)
+        ],
+        tile_counts,
+        pltpu.with_memory_space_constraint(cotangent, pltpu.HBM),
+    )
     gb = gb.reshape(hidden)
     if not fused_weight:
         gw = lax.psum(gw, ("row", "col"))

time: 40.4 us -> 31.3 us (0.77)
  local copies, waits for them, and re-layouts: 9.07 us -> 2.46 us
  Pallas kernels: 29.7 us -> 27.3 us
    unnamed x18 -> x4, local copies, waits for them, and re-layouts: 9.07 us -> 2.46 us
    pallas_call x1, Pallas kernels: 29.7 us -> 27.3 us  [shards(): pl.pallas_call(functools.partial(kernel, n_row, n_col, fused_weight), out...]
where the time goes in v2:
time: 31.3 us; the launch traced here: 31.1 us
  Pallas kernels  27.3 us (87%)
  local copies, waits for them, and re-layouts  2.46 us (8%)
  between operations  1.29 us (4%)
    pallas_call x1, Pallas kernels, shards(): pl.pallas_call(functools.partial(kernel, n_row, n_col, fused_weight), out...  27.3 us
    unnamed x4, local copies, waits for them, and re-layouts  2.46 us

profile of v2, /device:TPU:0, one launch (start us, length us, event | category | flops | bytes accessed | tf_op | source)
XLA Modules:
  0.0 31.1 jit_solution(9211633929216090893)
XLA Ops:
  1.3 27.3 %shard_map.111 = (bf16[128,256]{1,0:T(8,128)(2,1)S(1)}, bf16[128,128]{1,0:T(8,128)(2,1)S(1)}, f32[128,256]{1,0:T(8,128)S(1)}, f32[1,256]{1,0:T(1,128)S(1)}) custom-call(bf16[128,128]{1,0:T(8,128)(2,1)} %feat_hbm.1, bf16[128,256]{1,0:T(8,128)(2,1)} %weight_hbm.1, f32[1,256]{1,0:T(1,128)} %bitcast.3, bf16[1,1,8,512,512]{4,3,2,1,0:T(8,128)(2,1)} %tiles_hbm.1, ...), custom_call_target="tpu_custom_call" | custom-call | tf_op jit(solution)/shard_map/pallas_call | solution.py:261
  28.6 0.6 %copy.17 = bf16[128,256]{1,0:T(8,128)(2,1)} copy(bf16[128,256]{1,0:T(8,128)(2,1)S(1)} %get-tuple-element.16) | data formatting | bytes 131072
  29.3 0.6 %copy.18 = bf16[128,128]{1,0:T(8,128)(2,1)} copy(bf16[128,128]{1,0:T(8,128)(2,1)S(1)} %get-tuple-element.17) | data formatting | bytes 65536
  29.9 0.7 %copy.19 = f32[128,256]{1,0:T(8,128)} copy(f32[128,256]{1,0:T(8,128)S(1)} %get-tuple-element.18) | data formatting | bytes 262144
  30.5 0.6 %copy.20 = f32[256]{0:T(256)} copy(f32[256]{0:T(256)S(1)} %bitcast.2) | data formatting | bytes 2048

commit v3 on v2

--- a/solution.py
+++ b/solution.py
@@ -247,6 +247,16 @@
         wait_out(gw_in.at[pl.ds(0, n_row - 1)], 4)
         wait_out(gw_mid.at[pl.ds(0, n_col - 1)], 5)
         wait_out(gw_all.at[pl.ds(0, n_row - 1)], 6)
+
+
+def write_out(*refs):
+    count = (len(refs) - 1) // 2
+    sems = refs[-1]
+    copies = [pltpu.make_async_copy(refs[i], refs[count + i], sems.at[i]) for i in range(count)]
+    for copy in copies:
+        copy.start()
+    for copy in copies:
+        copy.wait()
 
 
 def shards(n_row, n_col, features, weight, bias, tiles, tile_rows, tile_cols, tile_counts, cotangent):
@@ -305,6 +315,15 @@
         tile_counts,
         pltpu.with_memory_space_constraint(cotangent, pltpu.HBM),
     )
+    results = (out, gf, gw, gb)
+    out, gf, gw, gb = pl.pallas_call(
+        write_out,
+        out_shape=tuple(jax.ShapeDtypeStruct(x.shape, x.dtype) for x in results),
+        in_specs=[vmem] * 4,
+        out_specs=(pl.BlockSpec(memory_space=pltpu.HBM),) * 4,
+        scratch_shapes=[pltpu.SemaphoreType.DMA((4,))],
+        compiler_params=pltpu.CompilerParams(vmem_limit_bytes=2 * 1024 * 1024),
+    )(*results)
     gb = gb.reshape(hidden)
     if not fused_weight:
         gw = lax.psum(gw, ("row", "col"))

time: 31.3 us -> 29.5 us (0.942)
  local copies, waits for them, and re-layouts: 2.46 us -> 0 us
  Pallas kernels: 27.3 us -> 28.1 us
    unnamed x4 -> x0, local copies, waits for them, and re-layouts: 2.46 us -> none
    pallas_call x0 -> x1, Pallas kernels: none -> 0.73 us  [shards(): pl.pallas_call(write_out, out_shape=tuple((jax.ShapeDtypeStruct(x.shape,...]
where the time goes in v3:
time: 29.5 us; the launch traced here: 29.4 us
  Pallas kernels  28.1 us (95%)
  between operations  1.29 us (4%)
    pallas_call x1, Pallas kernels, shards(): pl.pallas_call(functools.partial(kernel, n_row, n_col, fused_weight), out...  27.3 us
    pallas_call x1, Pallas kernels, shards(): pl.pallas_call(write_out, out_shape=tuple((jax.ShapeDtypeStruct(x.shape,...  0.73 us

profile of v3, /device:TPU:0, one launch (start us, length us, event | category | flops | bytes accessed | tf_op | source)
XLA Modules:
  0.0 29.4 jit_solution(13308864048845817269)
XLA Ops:
  1.3 27.3 %shard_map.111 = (bf16[128,256]{1,0:T(8,128)(2,1)S(1)}, bf16[128,128]{1,0:T(8,128)(2,1)S(1)}, f32[128,256]{1,0:T(8,128)S(1)}, f32[1,256]{1,0:T(1,128)S(1)}) custom-call(bf16[128,128]{1,0:T(8,128)(2,1)} %feat_hbm.1, bf16[128,256]{1,0:T(8,128)(2,1)} %weight_hbm.1, f32[1,256]{1,0:T(1,128)} %bitcast.2, bf16[1,1,8,512,512]{4,3,2,1,0:T(8,128)(2,1)} %tiles_hbm.1, ...), custom_call_target="tpu_custom_call" | custom-call | tf_op jit(solution)/shard_map/pallas_call | solution.py:271
  28.6 0.7 %shard_map.112 = (bf16[128,256]{1,0:T(8,128)(2,1)}, bf16[128,128]{1,0:T(8,128)(2,1)}, f32[128,256]{1,0:T(8,128)}, f32[1,256]{1,0:T(1,128)}) custom-call(bf16[128,256]{1,0:T(8,128)(2,1)S(1)} %get-tuple-element.12.refs_0_, bf16[128,128]{1,0:T(8,128)(2,1)S(1)} %get-tuple-element.13.refs_1_, f32[128,256]{1,0:T(8,128)S(1)} %get-tuple-element.14.refs_2_, ...), custom_call_target="tpu_custom_call" | custom-call | tf_op jit(solution)/shard_map/pallas_call | solution.py:319
